TPU v7x, 32 devices: a whole 2x2x4 slice. The times are simulated.
32 devices in a mesh: dp: 16 (over z, y, core), tensor: 2 (over x).
Axes of the slice: x: 2, y: 2, z: 4, core: 2. Of those that a mesh axis runs over, the one named last changes fastest.
Arguments:
- train_hidden: bfloat16 [16, 128, 28672], P('dp', None, 'tensor'), may hold values from -6 to 6
- train_grad: bfloat16 [16, 128, 8192], P('dp', None, 'tensor'), may hold values from -6 to 6
- test_hidden: bfloat16 [16, 64, 28672], P('dp', None, 'tensor'), may hold values from -6 to 6
- test_grad: bfloat16 [16, 64, 8192], P('dp', None, 'tensor'), may hold values from -6 to 6
- proj_in: bfloat16 [64, 28672], P(None, 'tensor'), may hold values from -0.03125 to 0.03125
- proj_out: bfloat16 [64, 8192], P(None, 'tensor'), may hold values from -0.0625 to 0.0625
- precond_in: float32 [64, 64], replicated, may hold values from -0.75 to 0.75
- precond_out: float32 [64, 64], replicated, may hold values from -0.75 to 0.75
Outputs:
- scores: float32 [16, 16], P('dp', 'tensor')
All inputs are finite; a program needn't handle non-finite values.
Results may differ from a plain program's by a relative error of at most 0.0029.
Values may be sent and summed in bfloat16 or wider, within the bound.
A program may use at most 64 MiB of HBM per device.

v0:
```python
import functools
import math

import jax
import jax.numpy as jnp
from jax import lax
from jax.experimental import pallas as pl
from jax.experimental.pallas import tpu as pltpu
from jax.sharding import PartitionSpec as P

MESH = pl.DeviceIdType.MESH


def each(low, high, step):
    if high - low <= 16:
        for k in range(low, high):
            step(k)
    else:
        lax.fori_loop(low, high, lambda k, _: (step(k), 0)[1], 0)


def project(rows, factor):
    return lax.dot_general(
        rows, factor, (((1,), (1,)), ((), ())), preferred_element_type=jnp.float32
    )


def hi_lo(x):
    hi = x.astype(jnp.bfloat16)
    return hi, (x - hi.astype(jnp.float32)).astype(jnp.bfloat16)


def hi_beside_lo(twins):
    hi, lo = hi_lo(twins)
    lane = lax.broadcasted_iota(jnp.int32, twins.shape, 1)
    return jnp.where(lane < twins.shape[1] // 2, hi.astype(jnp.float32), lo.astype(jnp.float32)).astype(
        jnp.bfloat16
    )


def twins(x):
    return jnp.concatenate([x, x], axis=1)


def fold_twins(y):
    width = y.shape[1] // 2
    while width > 64:
        y = y[:, :width] + y[:, width:]
        width //= 2
    return y + jnp.concatenate([y[:, width:], y[:, :width]], axis=1)


def dot(a, b):
    return jnp.dot(a, b, preferred_element_type=jnp.float32)


def fold_rows(y):
    height = y.shape[0] // 2
    return y[:height] + y[height:]


def pack(own, fold):
    rows, lanes = own.shape
    if fold == 1:
        return own[:, : lanes // 2]
    lane = lax.broadcasted_iota(jnp.int32, (rows // 2, lanes), 1)
    return jnp.where(lane < lanes // 2, own[: rows // 2], own[rows // 2 :])


def kernel(
    n_dp, n_tensor, chunks, fold, factor,
    th_hbm, tg_hbm, qh_hbm, qg_hbm, pi_hbm, po_hbm, ci_hbm, co_hbm,
    out_ref,
    th, tg, qh, qg, pi, po, ci, co,
    rq_own, rq_in, rt_own, rt_in, lq_own, lq_in, lt_own, lt_in, gathered, part, part_in,
    load_sem, pi_sem, qh_sem, th_sem,
    rq_send, rq_recv, rt_send, rt_recv, lq_send, lq_recv, lt_send, lt_recv,
    g_send, g_recv, p_send, p_recv,
):
    me_dp = lax.axis_index("dp")
    me_t = lax.axis_index("tensor")
    hid = pi.shape[1]
    step = hid // chunks

    def load(src, dst, sem):
        return pltpu.make_async_copy(src, dst, sem)

    def piece(c):
        return pl.ds(pl.multiple_of(c * step, step), step)

    po_load = load(po_hbm, po, load_sem.at[0])
    qg_load = load(qg_hbm, qg, load_sem.at[1])
    tg_load = load(tg_hbm, tg, load_sem.at[2])
    ci_load = load(ci_hbm, ci, load_sem.at[3])
    co_load = load(co_hbm, co, load_sem.at[4])
    pi_load = lambda c: load(pi_hbm.at[:, piece(c)], pi.at[:, piece(c)], pi_sem.at[c])
    qh_load = lambda c: load(qh_hbm.at[:, :, piece(c)], qh.at[:, :, piece(c)], qh_sem.at[c])
    th_load = lambda c: load(th_hbm.at[:, :, piece(c)], th.at[:, :, piece(c)], th_sem.at[c])

    po_load.start()
    qg_load.start()

    barrier = pltpu.get_barrier_semaphore()

    def greet_tensor(k):
        peer = lax.rem(me_t + k, n_tensor)
        pl.semaphore_signal(barrier, inc=1, device_id={"tensor": peer}, device_id_type=MESH)

    def greet_dp(k):
        peer = lax.rem(me_dp + k, n_dp)
        pl.semaphore_signal(barrier, inc=1, device_id={"dp": peer}, device_id_type=MESH)

    for c in range(chunks):
        pi_load(c).start()
        qh_load(c).start()
    co_load.start()
    ci_load.start()
    each(1, n_tensor, greet_tensor)
    each(1, n_dp, greet_dp)
    def swap(own, landing, send, recv, k, shared):
        peer = lax.rem(me_t + k, n_tensor)
        return pltpu.make_async_remote_copy(
            src_ref=own if shared else own.at[peer],
            dst_ref=landing.at[k - 1],
            send_sem=send.at[k - 1],
            recv_sem=recv.at[k - 1],
            device_id={"tensor": peer},
            device_id_type=MESH,
        )

    rq_swap = lambda k: swap(rq_own, rq_in, rq_send, rq_recv, k, True)
    rt_swap = lambda k: swap(rt_own, rt_in, rt_send, rt_recv, k, True)
    lq_swap = lambda k: swap(lq_own, lq_in, lq_send, lq_recv, k, False)
    lt_swap = lambda k: swap(lt_own, lt_in, lt_send, lt_recv, k, False)

    def spread(k):
        return pltpu.make_async_remote_copy(
            src_ref=gathered.at[me_dp],
            dst_ref=gathered.at[me_dp],
            send_sem=g_send,
            recv_sem=g_recv,
            device_id={"dp": lax.rem(me_dp + k, n_dp)},
            device_id_type=MESH,
        )

    every_other = pltpu.make_async_remote_copy(
        src_ref=gathered.at[pl.ds(0, n_dp - 1)],
        dst_ref=gathered.at[pl.ds(0, n_dp - 1)],
        send_sem=g_send,
        recv_sem=g_recv,
        device_id={"dp": lax.rem(me_dp + 1, n_dp)},
        device_id_type=MESH,
    )

    def summed(own, landing, one_swap):
        total = own
        for k in range(1, n_tensor):
            one_swap(k).wait_recv()
            total = total + landing[k - 1]
        return total

    rank = ci.shape[0]
    rows = rank // n_tensor

    po_load.wait()
    qg_load.wait()
    tg_load.start()
    rq_own[...] = hi_beside_lo(twins(project(qg[0], po[...])))
    def query_chunk(c, total):
        pi_load(c).wait()
        qh_load(c).wait()
        th_load(c).start()
        return total + project(pi[:, piece(c)], qh[0, :, piece(c)])

    left = lax.fori_loop(
        0, chunks, query_chunk, jnp.zeros((rank, qh.shape[1]), jnp.float32)
    )
    ci_load.wait()
    ci_parts = jnp.concatenate(hi_lo(ci[...]), axis=0)
    left = fold_rows(dot(ci_parts, hi_beside_lo(twins(left))))
    left = hi_beside_lo(fold_twins(left))
    for t in range(n_tensor):
        lq_own[t] = left[t * rows : (t + 1) * rows]
    pl.semaphore_wait(barrier, n_dp + n_tensor - 2)
    for k in range(1, n_tensor):
        lq_swap(k).start()
        rq_swap(k).start()

    tg_load.wait()
    rt_own[...] = hi_beside_lo(twins(project(tg[0], po[...])))
    for k in range(1, n_tensor):
        rt_swap(k).start()

    co_load.wait()
    co_parts = hi_beside_lo(twins(co[...]))
    co_parts = jnp.concatenate([co_parts, co_parts], axis=0)
    right = dot(rq_own[...], co_parts)
    for k in range(1, n_tensor):
        rq_swap(k).wait_recv()
        right = right + dot(rq_in[k - 1], co_parts)
    right = hi_beside_lo(fold_twins(right))
    right = jnp.concatenate([right] * (2 * n_tensor), axis=0)

    def example_chunk(c, total):
        th_load(c).wait()
        return total + project(pi[:, piece(c)], th[0, :, piece(c)])

    before = chunks // 2
    example = lax.fori_loop(
        0, before, example_chunk, jnp.zeros((rank, th.shape[1]), jnp.float32)
    )

    lefts = [lq_own[me_t]]
    for k in range(1, n_tensor):
        lq_swap(k).wait_recv()
        lefts.append(lq_in[k - 1])
    conditioned = fold_twins(dot(jnp.concatenate(lefts, axis=1), right))
    gathered[me_dp] = pack(conditioned, fold).astype(gathered.dtype)
    each(1, n_dp, lambda k: spread(k).start())

    example = lax.fori_loop(before, chunks, example_chunk, example)
    for t in range(n_tensor):
        lt_own[t] = example[t * rows : (t + 1) * rows]
    for k in range(1, n_tensor):
        lt_swap(k).start()

    rights = [rt_own[...]]
    for k in range(1, n_tensor):
        rt_swap(k).wait_recv()
        rights.append(rt_in[k - 1])
    rights = jnp.concatenate(rights, axis=1)
    mine = jnp.concatenate(hi_lo(summed(lt_own[me_t], lt_in, lt_swap)), axis=0)
    share = pack(fold_twins(fold_rows(dot(mine, rights))), fold)

    every_other.wait_recv()
    lanes = jnp.sum(gathered[...].astype(jnp.float32) * share[None], axis=1)
    part[...] = lanes.reshape(part.shape)
    p_swap = lambda k: swap(part, part_in, p_send, p_recv, k, False)
    for k in range(1, n_tensor):
        p_swap(k).start()
    total = summed(part[me_t], part_in, p_swap)
    out_ref[...] = jnp.sum(total.T, axis=0, keepdims=True) * factor

    for one_swap in (rq_swap, rt_swap, lq_swap, lt_swap, p_swap):
        for k in range(1, n_tensor):
            one_swap(k).wait_send()
    every_other.wait_send()


def shards(n_dp, n_tensor, th, tg, qh, qg, pi, po, ci, co):
    rank, hid = pi.shape
    seq, qry = th.shape[1], qh.shape[1]
    share = rank // n_tensor
    fold = 2 if share % 32 == 0 else 1
    packed = (share // fold, rank * fold)
    kept = n_dp // n_tensor
    chunks = 4
    f32, bf16 = jnp.float32, jnp.bfloat16
    dma = pltpu.SemaphoreType.DMA
    others = n_tensor - 1
    factor = 1.0 / (rank * math.sqrt(seq * qry))
    args = (th, tg, qh, qg, pi, po, ci, co)
    pair = dma((others,))
    rows = (seq + qry) * rank * 2
    return pl.pallas_call(
        functools.partial(kernel, n_dp, n_tensor, chunks, fold, factor),
        out_shape=jax.ShapeDtypeStruct((1, kept), f32),
        in_specs=[pl.BlockSpec(memory_space=pltpu.HBM)] * len(args),
        out_specs=pl.BlockSpec(memory_space=pltpu.VMEM),
        scratch_shapes=[pltpu.VMEM(a.shape, a.dtype) for a in args]
        + [
            pltpu.VMEM((qry, 2 * rank), bf16),
            pltpu.VMEM((others, qry, 2 * rank), bf16),
            pltpu.VMEM((seq, 2 * rank), bf16),
            pltpu.VMEM((others, seq, 2 * rank), bf16),
            pltpu.VMEM((n_tensor, share, 2 * rank), bf16),
            pltpu.VMEM((others, share, 2 * rank), bf16),
            pltpu.VMEM((n_tensor, share, seq), f32),
            pltpu.VMEM((others, share, seq), f32),
            pltpu.VMEM((n_dp,) + packed, bf16),
            pltpu.VMEM((n_tensor, kept, packed[1]), f32),
            pltpu.VMEM((others, kept, packed[1]), f32),
            dma((5,)), dma((chunks,)), dma((chunks,)), dma((chunks,)),
        ]
        + [pair] * 8
        + [dma, dma, pair, pair],
        cost_estimate=pl.CostEstimate(
            flops=rows * (hid + po.shape[1]),
            bytes_accessed=sum(a.size * a.dtype.itemsize for a in args),
            transcendentals=0,
        ),
        compiler_params=pltpu.CompilerParams(
            collective_id=0, has_side_effects=True, vmem_limit_bytes=60 * 1024 * 1024
        ),
    )(*args)


def solution(mesh):
    placed = (
        P("dp", None, "tensor"),
        P("dp", None, "tensor"),
        P("dp", None, "tensor"),
        P("dp", None, "tensor"),
        P(None, "tensor"),
        P(None, "tensor"),
        P(),
        P(),
    )
    body = functools.partial(shards, mesh.shape["dp"], mesh.shape["tensor"])
    return jax.shard_map(
        body, mesh=mesh, in_specs=placed, out_specs=P("dp", "tensor"), check_vma=False
    )
```

profile of v0, /device:TPU:0, one launch (start us, length us, event | category | flops | bytes accessed | tf_op | source)
XLA Modules:
  0.0 19.7 jit_solution(15219423547365499983)
XLA Ops:
  0.0 18.5 %shard_map.82 = f32[1,8]{1,0:T(1,128)} custom-call(bf16[1,128,14336]{2,1,0:T(8,128)(2,1)} %th_hbm.1, bf16[1,128,4096]{2,1,0:T(8,128)(2,1)} %tg_hbm.1, bf16[1,64,14336]{2,1,0:T(8,128)(2,1)} %qh_hbm.1, bf16[1,64,4096]{2,1,0:T(8,128)(2,1)} %qg_hbm.1, bf16[64,14336]{1,0:T(8,128)(2,1)} %pi_hbm.1, bf16[64,4096]{1,0:T(8,128)(2,1)} %po_hbm.1, f32[64,64]{1,0:T(8,128)} %ci_hbm.1, ...), custom_call_target="tpu_custom_call" | custom-call | flops 452984832 | bytes 9469952 | tf_op jit(solution)/shard_map/pallas_call | solution.py:265
  18.5 1.2 %copy.10 = f32[1,8]{1,0:T(1,128)} copy(f32[1,8]{1,0:T(1,128)} %shard_map.82) | data formatting | bytes 64
where the time goes:
time: 19.9 us; the launch traced here: 19.7 us
  Pallas kernels  18.5 us (93%)
  local copies, waits for them, and re-layouts  1.19 us (6%)
    pallas_call x1, Pallas kernels, shards(): pl.pallas_call(functools.partial(kernel, n_dp, n_tensor, chunks, fold, fa...  18.5 us
    unnamed x1, local copies, waits for them, and re-layouts  1.19 us

commit v1 on v0

--- a/solution.py
+++ b/solution.py
@@ -113,8 +113,11 @@
     for c in range(chunks):
         pi_load(c).start()
         qh_load(c).start()
+    ci_load.start()
     co_load.start()
-    ci_load.start()
+    tg_load.start()
+    for c in range(chunks):
+        th_load(c).start()
     each(1, n_tensor, greet_tensor)
     each(1, n_dp, greet_dp)
     def swap(own, landing, send, recv, k, shared):
@@ -164,12 +167,10 @@
 
     po_load.wait()
     qg_load.wait()
-    tg_load.start()
     rq_own[...] = hi_beside_lo(twins(project(qg[0], po[...])))
     def query_chunk(c, total):
         pi_load(c).wait()
         qh_load(c).wait()
-        th_load(c).start()
         return total + project(pi[:, piece(c)], qh[0, :, piece(c)])
 
     left = lax.fori_loop(

time: 19.9 us -> 20.3 us (1.020)
  Pallas kernels: 18.5 us -> 19 us
    pallas_call x1, Pallas kernels: 18.5 us -> 19 us  [shards(): pl.pallas_call(functools.partial(kernel, n_dp, n_tensor, chunks, fold, fa...]
where the time goes in v1:
time: 20.3 us; the launch traced here: 20.2 us
  Pallas kernels  19 us (94%)
  local copies, waits for them, and re-layouts  1.19 us (6%)
    pallas_call x1, Pallas kernels, shards(): pl.pallas_call(functools.partial(kernel, n_dp, n_tensor, chunks, fold, fa...  19 us
    unnamed x1, local copies, waits for them, and re-layouts  1.19 us

profile of v1, /device:TPU:0, one launch (start us, length us, event | category | flops | bytes accessed | tf_op | source)
XLA Modules:
  0.0 20.2 jit_solution(4897252646786413279)
XLA Ops:
  0.0 19.0 %shard_map.82 = f32[1,8]{1,0:T(1,128)} custom-call(bf16[1,128,14336]{2,1,0:T(8,128)(2,1)} %th_hbm.1, bf16[1,128,4096]{2,1,0:T(8,128)(2,1)} %tg_hbm.1, bf16[1,64,14336]{2,1,0:T(8,128)(2,1)} %qh_hbm.1, bf16[1,64,4096]{2,1,0:T(8,128)(2,1)} %qg_hbm.1, bf16[64,14336]{1,0:T(8,128)(2,1)} %pi_hbm.1, bf16[64,4096]{1,0:T(8,128)(2,1)} %po_hbm.1, f32[64,64]{1,0:T(8,128)} %ci_hbm.1, ...), custom_call_target="tpu_custom_call" | custom-call | flops 452984832 | bytes 9469952 | tf_op jit(solution)/shard_map/pallas_call | solution.py:266
  19.0 1.2 %copy.10 = f32[1,8]{1,0:T(1,128)} copy(f32[1,8]{1,0:T(1,128)} %shard_map.82) | data formatting | bytes 64

commit v2 on v0

--- a/solution.py
+++ b/solution.py
@@ -205,7 +205,7 @@
         th_load(c).wait()
         return total + project(pi[:, piece(c)], th[0, :, piece(c)])
 
-    before = chunks // 2
+    before = chunks // 4
     example = lax.fori_loop(
         0, before, example_chunk, jnp.zeros((rank, th.shape[1]), jnp.float32)
     )

time: 19.9 us -> 19.8 us (level)
  no operation moved by 1% of the time
where the time goes in v2:
time: 19.8 us; the launch traced here: 19.7 us
  Pallas kernels  18.5 us (93%)
  local copies, waits for them, and re-layouts  1.19 us (6%)
    pallas_call x1, Pallas kernels, shards(): pl.pallas_call(functools.partial(kernel, n_dp, n_tensor, chunks, fold, fa...  18.5 us
    unnamed x1, local copies, waits for them, and re-layouts  1.19 us

profile of v2, /device:TPU:0, one launch (start us, length us, event | category | flops | bytes accessed | tf_op | source)
XLA Modules:
  0.0 19.7 jit_solution(11202276602477985103)
XLA Ops:
  0.0 18.5 %shard_map.82 = f32[1,8]{1,0:T(1,128)} custom-call(bf16[1,128,14336]{2,1,0:T(8,128)(2,1)} %th_hbm.1, bf16[1,128,4096]{2,1,0:T(8,128)(2,1)} %tg_hbm.1, bf16[1,64,14336]{2,1,0:T(8,128)(2,1)} %qh_hbm.1, bf16[1,64,4096]{2,1,0:T(8,128)(2,1)} %qg_hbm.1, bf16[64,14336]{1,0:T(8,128)(2,1)} %pi_hbm.1, bf16[64,4096]{1,0:T(8,128)(2,1)} %po_hbm.1, f32[64,64]{1,0:T(8,128)} %ci_hbm.1, ...), custom_call_target="tpu_custom_call" | custom-call | flops 452984832 | bytes 9469952 | tf_op jit(solution)/shard_map/pallas_call | solution.py:265
  18.5 1.2 %copy.10 = f32[1,8]{1,0:T(1,128)} copy(f32[1,8]{1,0:T(1,128)} %shard_map.82) | data formatting | bytes 64
